TPU v7x, 512 devices: a whole 4x8x8 slice. The times are simulated.
512 devices in a mesh: dp: 2 (over x_hi), ffn: 16 (over z, core), hid: 16 (over y, x_lo).
Axes of the slice: x: 4 (x_hi: 2, x_lo: 2; x = x_hi * 2 + x_lo), y: 8, z: 8, core: 2. Of those that a mesh axis runs over, the one named last changes fastest.
Arguments:
- stream: bfloat16 [512, 16384], P('dp', 'hid'), may hold values from -160 to 160
- steering: float32 [16384], P('hid'), may hold values from -40 to 40
- strength: float32 [512], P('dp'), may hold values from 0.5 to 2
- norm_gain_vector: float32 [16384], P('hid'), may hold values from 0.25 to 1.75
- frozen_weights: bfloat16 [2, 16384, 26624], P('dp', 'hid', 'ffn'), may hold values from -0.046875 to 0.046875
- adapter_down_factors: bfloat16 [2, 16384, 16], P(None, 'hid'), may hold values from -0.046875 to 0.046875
- adapter_up_factors: bfloat16 [2, 16, 26624], P(None, None, 'ffn'), may hold values from -1.5 to 1.5
- cotangent: bfloat16 [512, 26624], P(('dp', 'hid'), 'ffn'), may hold values from -6 to 6
Outputs:
- residual_stream_gradient: bfloat16 [512, 16384], P('dp', 'hid')
- steering_vector_gradient: float32 [16384], P('hid')
- adapter_down_gradient: float32 [2, 16384, 16], P(None, 'hid')
- adapter_up_gradient: float32 [2, 16, 26624], P(None, None, 'ffn')
All inputs are finite; a program needn't handle non-finite values.
Results may differ from a plain program's by a relative error of at most 0.0068.
Values may be sent and summed in bfloat16 or wider, within the bound.
A program may use at most 64 MiB of HBM per device.

v0:
```python
import jax
import jax.numpy as jnp
from jax import lax
from jax.sharding import PartitionSpec as P

MODEL_WIDTH = 16384
ADAPTER_SCALE = 0.5


def gated_layer_backward(
    preactivation_values, adapter_input_rows, adapter_up_factors, incoming_gradient
):
    activation_values = preactivation_values + ADAPTER_SCALE * jnp.einsum(
        "dch,chn->dcn", adapter_input_rows, adapter_up_factors, preferred_element_type=jnp.float32
    )
    gate_values = activation_values[:, 0]
    up_projection_values = activation_values[:, 1]
    sigma = jax.nn.sigmoid(gate_values)
    flow = incoming_gradient.astype(jnp.float32)
    gate_grad = flow * up_projection_values * sigma * (1.0 + gate_values * (1.0 - sigma))
    upper_grad = flow * gate_values * sigma
    return jnp.stack([gate_grad, upper_grad], axis=1).astype(jnp.bfloat16)


def local(
    stream,
    steering,
    strength,
    norm_gain_vector,
    frozen_weights,
    adapter_down_factors,
    adapter_up_factors,
    cotangent,
):
    rows = stream.astype(jnp.float32)
    row_squares = jnp.sum(rows * rows, axis=1)
    steer_power = jnp.sum(steering * steering)
    total_rows, total_steer = lax.psum((row_squares, steer_power), "hid")
    stream_ms = total_rows / MODEL_WIDTH + 1e-06
    steer_ms = total_steer / MODEL_WIDTH + 1e-06
    scale = strength * jnp.sqrt(stream_ms / steer_ms)
    steered = rows + scale[:, None] * steering[None, :]
    steered_power = lax.psum(jnp.sum(steered * steered, axis=1), "hid")
    inv_rms = lax.rsqrt(steered_power / MODEL_WIDTH + 1e-05)
    normalized_input = (steered * inv_rms[:, None] * norm_gain_vector[None, :]).astype(jnp.bfloat16)
    down_piece = jnp.einsum(
        "jq,hqp->jhp", normalized_input, adapter_down_factors, preferred_element_type=jnp.float32
    )
    weights = lax.all_gather(frozen_weights, "dp", axis=0, tiled=True)
    full_acts = jnp.einsum(
        "td,kdf->tkf", normalized_input, weights, preferred_element_type=jnp.float32
    )
    preactivation_values, adapter_sum = lax.psum((full_acts, down_piece), "hid")
    incoming_gradient = lax.all_gather(cotangent, "hid", axis=0, tiled=True)
    adapter_input_rows = adapter_sum.astype(jnp.bfloat16)
    activation_gradient = gated_layer_backward(
        preactivation_values, adapter_input_rows, adapter_up_factors, incoming_gradient
    )
    grad_share = lax.psum_scatter(
        jnp.einsum("tkf,kdf->td", activation_gradient, weights, preferred_element_type=jnp.float32),
        "ffn",
        scatter_dimension=0,
        tiled=True,
    )
    input_frozen_term = lax.all_gather(grad_share, "ffn", axis=0, tiled=True)
    backward_piece = jnp.einsum(
        "sua,uqa->suq", activation_gradient, adapter_up_factors, preferred_element_type=jnp.float32
    )
    back_sum = lax.psum(backward_piece, "ffn")
    lowrank_backward = back_sum.astype(jnp.bfloat16)
    normalized_gradient = input_frozen_term + ADAPTER_SCALE * jnp.einsum(
        "qme,mfe->qf", lowrank_backward, adapter_down_factors, preferred_element_type=jnp.float32
    )
    product = (
        lax.psum(jnp.sum(steered * norm_gain_vector[None, :] * normalized_gradient, axis=1), "hid")
        / MODEL_WIDTH
    )
    steered_grad = (
        inv_rms[:, None] * norm_gain_vector[None, :] * normalized_gradient
        - (inv_rms**3 * product)[:, None] * steered
    )
    residual_stream_gradient = steered_grad.astype(jnp.bfloat16)
    steering_part = jnp.sum(scale[:, None] * steered_grad, axis=0)
    down_projection_gradient = ADAPTER_SCALE * jnp.einsum(
        "cl,can->aln", normalized_input, lowrank_backward, preferred_element_type=jnp.float32
    )
    up_projection_gradient = ADAPTER_SCALE * jnp.einsum(
        "qyj,qyi->yji", adapter_input_rows, activation_gradient, preferred_element_type=jnp.float32
    )
    down_projection_gradient, up_projection_gradient, steering_vector_gradient = lax.psum(
        (down_projection_gradient, up_projection_gradient, steering_part), "dp"
    )
    return (
        residual_stream_gradient,
        steering_vector_gradient,
        down_projection_gradient,
        up_projection_gradient,
    )


def solution(mesh):
    in_specs = (
        P("dp", "hid"),
        P("hid"),
        P("dp"),
        P("hid"),
        P("dp", "hid", "ffn"),
        P(None, "hid", None),
        P(None, None, "ffn"),
        P(("dp", "hid"), "ffn"),
    )
    out_specs = (P("dp", "hid"), P("hid"), P(None, "hid", None), P(None, None, "ffn"))
    return jax.shard_map(local, mesh=mesh, in_specs=in_specs, out_specs=out_specs, check_vma=False)
```

profile of v0, /device:TPU:1, one launch (start us, length us, event | category | flops | bytes accessed | tf_op | source)
XLA Modules:
  0.0 484.7 jit_solution(4777915458065586716)
XLA Ops:
  8.8 29.3 %all-reduce = (f32[256]{0:T(256)S(1)}, f32[]{:T(128)}) all-reduce(f32[256]{0:T(256)S(1)} %fusion.8, f32[]{:T(128)} %multiply_reduce_fusion.3), channel_id=1, replica_groups=mesh['dp'=2,'ffn'=16,'hid'=16] {'hid'}, use_global_device_ids=true, to_apply=%region_1.0 | all-reduce | flops 257 | bytes 2056 | tf_op jit(solution)/shard_map/psum | solution.py:38
  39.1 25.7 %psum.72 = f32[256]{0:T(256)S(1)} all-reduce(f32[256]{0:T(256)S(1)} %multiply_reduce_fusion.2), channel_id=1, replica_groups=mesh['dp'=2,'ffn'=16,'hid'=16] {'hid'}, use_global_device_ids=true, to_apply=%region_5.0 | all-reduce | flops 256 | bytes 2048 | tf_op jit(solution)/shard_map/psum | solution.py:43
  65.1 47.6 %all-gather.3.cloned.1.call-done = bf16[2,1024,1664]{2,1,0:T(8,128)(2,1)} async-done(((bf16[1,1024,1664]{2,1,0:T(8,128)(2,1)}), bf16[2,1024,1664]{2,1,0:T(8,128)(2,1)}) %all-gather.3.cloned.1.call-update) | async-done | bytes 6815760 | tf_op jit(solution)/shard_map/all_gather | solution.py:49
  112.8 6.7 %fusion.12 = f32[256,2,1664]{2,0,1:T(8,128)} fusion(bf16[2,1024,1664]{2,1,0:T(8,128)(2,1)} %all-gather.3.cloned.1.call-done, bf16[256,1024]{1,0:T(8,128)(2,1)S(1)} %multiply_convert_fusion), kind=kOutput, calls=%fused_computation.31 | convolution fusion | flops 1744830464 | bytes 10747904 | tf_op jit(solution)/shard_map/td,kdf->tkf/dot_general | solution.py:50
  119.6 0.8 copy-done.4
  120.6 50.2 %psum.74 = bf16[256,2,16]{0,2,1:T(8,128)(2,1)S(1)} all-reduce(f32[256,2,16]{0,2,1:T(8,128)S(1)} %bitcast.55), channel_id=1, replica_groups=mesh['dp'=2,'ffn'=16,'hid'=16] {'hid'}, use_global_device_ids=true, to_apply=%region_7.0 | all-reduce | flops 8192 | bytes 49152 | tf_op jit(solution)/shard_map/psum | solution.py:53
  170.8 53.1 %all_gather.9 = bf16[256,1664]{1,0:T(8,128)(2,1)S(1)} all-gather(bf16[16,1664]{1,0:T(8,128)(2,1)S(1)} %copy-done.6), channel_id=1, replica_groups=mesh['dp'=2,'ffn'=16,'hid'=16] {'hid'}, dimensions={0}, use_global_device_ids=true | all-gather | bytes 905216 | tf_op jit(solution)/shard_map/all_gather | solution.py:54
  223.9 82.8 %all-reduce.5.cloned.1.call-done = f32[256,2,1664]{2,0,1:T(8,128)} async-done(((f32[256,2,1664]{2,0,1:T(8,128)}), f32[256,2,1664]{2,0,1:T(8,128)}) %all-reduce.5.cloned.1.call-update) | async-done | bytes 3407888 | tf_op jit(solution)/shard_map/psum | solution.py:53
  306.7 2.6 bitcast_add_fusion
  309.3 0.9 fusion.10
  310.2 1.0 copy-done.2
  311.2 5.9 %convolution_bitcast_fusion.1 = f32[256,1024]{1,0:T(8,128)} fusion(bf16[2,1024,1664]{2,1,0:T(8,128)(2,1)} %all-gather.3.cloned.1.call-done, bf16[256,1,1664]{2,0,1:T(8,128)(2,1)S(1)} %get-tuple-element.11, bf16[256,1,1664]{2,0,1:T(8,128)(2,1)S(1)} %get-tuple-element.10), kind=kOutput, calls=%fused_computation.16 | convolution fusion | flops 1745682432 | bytes 9568256 | tf_op jit(solution)/shard_map/tkf,kdf->td/dot_general | solution.py:60
  317.1 60.2 %reduce-scatter.2.cloned.1.call-done = f32[16,1024]{1,0:T(8,128)} async-done(((f32[256,1024]{1,0:T(8,128)}), f32[16,1024]{1,0:T(8,128)}) %reduce-scatter.2.cloned.1.call-update) | async-done | bytes 65552 | tf_op jit(solution)/shard_map/reduce_scatter | solution.py:59
  377.4 1.7 convolution_bitcast_fusion.2
  379.1 46.5 %psum.75 = bf16[256,2,16]{0,2,1:T(8,128)(2,1)S(1)} all-reduce(f32[256,2,16]{0,2,1:T(8,128)S(1)} %convolution_bitcast_fusion.2), channel_id=1, replica_groups=mesh['dp'=2,'ffn'=16,'hid'=16] {'ffn'}, use_global_device_ids=true, to_apply=%region_9.0 | all-reduce | flops 8192 | bytes 49152 | tf_op jit(solution)/shard_map/psum | solution.py:69
  425.6 1.1 convolution_multiply_fusion
  426.6 0.9 fusion.7
  427.6 1.7 multiply_reduce_fusion.1
  429.3 27.7 %psum.76 = f32[256]{0:T(256)S(1)} all-reduce(f32[256]{0:T(256)S(1)} %get-tuple-element.12), channel_id=1, replica_groups=mesh['dp'=2,'ffn'=16,'hid'=16] {'hid'}, use_global_device_ids=true, to_apply=%region_11.0 | all-reduce | flops 256 | bytes 2048 | tf_op jit(solution)/shard_map/psum | solution.py:75
  457.0 1.2 multiply_reduce_fusion
  458.2 5.9 %psum.77 = f32[1024]{0:T(1024)} all-reduce(f32[1024]{0:T(1024)S(1)} %get-tuple-element.8), channel_id=1, replica_groups=mesh['dp'=2,'ffn'=16,'hid'=16] {'dp'}, use_global_device_ids=true, to_apply=%region_13.0 | all-reduce | flops 1024 | bytes 8192 | tf_op jit(solution)/shard_map/psum | solution.py:90
  464.1 10.9 %all-reduce.7.cloned.1.call-done = (f32[2,1024,16]{1,2,0:T(8,128)}, f32[2,16,1664]{2,1,0:T(8,128)}) async-done(((f32[2,1024,16]{1,2,0:T(8,128)}, f32[2,16,1664]{2,1,0:T(8,128)}), (f32[2,1024,16]{1,2,0:T(8,128)}, f32[2,16,1664]{2,1,0:T(8,128)})) %all-reduce.7.cloned.1.call-update) | async-done | bytes 344080 | tf_op jit(solution)/shard_map/psum | solution.py:90
  475.0 1.6 copy.15
  476.5 1.6 copy.16
  (35 shorter events, 2.7 us)
Async XLA Ops:
  7.2 299.6 %copy-start = (bf16[2,16,1664]{2,1,0:T(8,128)(2,1)S(1)}, bf16[2,16,1664]{2,1,0:T(8,128)(2,1)}, u32[]{:S(2)}) copy-start(bf16[2,16,1664]{2,1,0:T(8,128)(2,1)} %param.14) | copy-start | bytes 319492
  7.2 0.8 copy-start.5
  7.2 1.4 copy-start.1
  7.2 31.6 %copy-start.8 = (f32[256]{0:T(256)S(1)}, f32[256]{0:T(256)}, u32[]{:S(2)}) copy-start(f32[256]{0:T(256)} %param.10) | copy-start | bytes 3076
  7.2 57.6 %copy-start.7 = (f32[1024]{0:T(1024)S(1)}, f32[1024]{0:T(1024)}, u32[]{:S(2)}) copy-start(f32[1024]{0:T(1024)} %param.11) | copy-start | bytes 12292
  7.2 105.6 %all-gather.3.cloned.1.call-start = ((), (), s32[]{:S(2)}) async-start(), calls=%async_computation.1 | async-start | bytes 10223616 | tf_op jit(solution)/shard_map/all_gather | solution.py:49
  8.0 298.8 %all-reduce.5.cloned.1.call-start = ((), (), s32[]{:S(2)}) async-start(), calls=%async_computation.2 | async-start | bytes 6815744 | tf_op jit(solution)/shard_map/psum | solution.py:53
  119.5 0.8 copy-start.4
  119.5 51.3 %copy-start.6 = (bf16[16,1664]{1,0:T(8,128)(2,1)S(1)}, bf16[16,1664]{1,0:T(8,128)(2,1)}, u32[]{:S(2)}) copy-start(bf16[16,1664]{1,0:T(8,128)(2,1)} %param.15) | copy-start | bytes 159748
  119.5 257.8 %reduce-scatter.2.cloned.1.call-start = ((), (), s32[]{:S(2)}) async-start(), calls=%async_computation.3 | async-start | bytes 1114112 | tf_op jit(solution)/shard_map/reduce_scatter | solution.py:59
  310.2 1.0 copy-start.2
  317.1 108.5 %copy-start.3 = (bf16[256,1,1664]{2,0,1:T(8,128)(2,1)S(1)}, bf16[256,1,1664]{2,0,1:T(8,128)(2,1)}, u32[]{:S(2)}) copy-start(bf16[256,1,1664]{2,0,1:T(8,128)(2,1)} %copy-done.2) | copy-start | bytes 2555908
  317.1 110.5 %all-gather.5.cloned.1.call-start = ((), (), s32[]{:S(2)}) async-start(), calls=%async_computation.4 | async-start | bytes 1114112 | tf_op jit(solution)/shard_map/all_gather | solution.py:65
  377.3 97.7 %all-reduce.7.cloned.1.call-start = ((), (), s32[]{:S(2)}) async-start(), calls=%async_computation.5 | async-start | bytes 688128 | tf_op jit(solution)/shard_map/psum | solution.py:90
Sparse Core Ops, SparseCore 0:
  10.1 102.5 all-gather.2
  119.6 187.0 all-reduce.4
  317.2 60.0 reduce-scatter.1
  379.3 43.0 all-gather.4
  427.7 47.2 all-reduce.6
where the time goes:
time: 485 us
  blocking collectives  238 us (49%)
  waiting for transfers between devices  202 us (42%)
  matrix products  20.7 us (4%)
  between operations  14.6 us (3%)
  local copies, waits for them, and re-layouts  4.97 us (1%)
    psum x1, waiting for transfers between devices, local(): preactivation_values, adapter_sum = lax.psum((full_acts, down_piece), 'hid')  82.8 us
    reduce_scatter x1, waiting for transfers between devices, local(): lax.psum_scatter(jnp.einsum('tkf,kdf->td', activation_gradient, weights,...  60.2 us
    all_gather x1, blocking collectives, local(): incoming_gradient = lax.all_gather(cotangent, 'hid', axis=0, tiled=True)  53.1 us
    psum x1, blocking collectives, local(): preactivation_values, adapter_sum = lax.psum((full_acts, down_piece), 'hid')  50.2 us
    all_gather x1, waiting for transfers between devices, local(): weights = lax.all_gather(frozen_weights, 'dp', axis=0, tiled=True)  47.6 us
    psum x1, blocking collectives, local(): back_sum = lax.psum(backward_piece, 'ffn')  46.5 us
    psum x1, blocking collectives, local(): total_rows, total_steer = lax.psum((row_squares, steer_power), 'hid')  29.3 us
    psum x1, blocking collectives, local(): lax.psum(jnp.sum(steered * norm_gain_vector[None, :] * normalized_gradien...  27.7 us
  transfers between devices with their start and end apart: 5, of which 4 were waited for; matrix products, arithmetic and copies ran while one was open for 2% of the time, Pallas kernels for 0%

commit v1 on v0

--- a/solution.py
+++ b/solution.py
@@ -46,7 +46,9 @@
     down_piece = jnp.einsum(
         "jq,hqp->jhp", normalized_input, adapter_down_factors, preferred_element_type=jnp.float32
     )
-    weights = lax.all_gather(frozen_weights, "dp", axis=0, tiled=True)
+    weights = jnp.concatenate(
+        lax.all_to_all(jnp.stack([frozen_weights] * lax.axis_size("dp")), "dp", 0, 0), axis=0
+    )
     full_acts = jnp.einsum(
         "td,kdf->tkf", normalized_input, weights, preferred_element_type=jnp.float32
     )

time: 485 us -> 535 us (1.10)
  blocking collectives: 238 us -> 301 us
  waiting for transfers between devices: 202 us -> 177 us
  starting transfers between devices: 0.2 us -> 6.75 us
  other arithmetic: 3.47 us -> 10 us
    psum x1, blocking collectives: 29.3 us -> 96.6 us  [local(): total_rows, total_steer = lax.psum((row_squares, steer_power), 'hid')]
    all_gather x1 -> x0, waiting for transfers between devices: 47.6 us -> none  [local(): weights = lax.all_gather(frozen_weights, 'dp', axis=0, tiled=True)]
    psum x1, waiting for transfers between devices: 82.8 us -> 105 us  [local(): preactivation_values, adapter_sum = lax.psum((full_acts, down_piece), 'hid')]
    all_to_all x0 -> x1, starting transfers between devices: none -> 6.59 us  [local(): lax.all_to_all(jnp.stack([frozen_weights] * lax.axis_size('dp')), 'dp', 0...]
    another operation x0 -> x1, other arithmetic: none -> 6.56 us  [local(): jnp.stack([frozen_weights] * lax.axis_size('dp'))]
  transfers between devices with their start and end apart: 5 -> 5, of which waited for: 4 -> 3; matrix products, arithmetic and copies ran while one was open for 2% -> 2% of each run, Pallas kernels for 0% -> 0%
where the time goes in v1:
time: 535 us
  blocking collectives  301 us (56%)
  waiting for transfers between devices  177 us (33%)
  matrix products  20.7 us (4%)
  between operations  14.5 us (3%)
  other arithmetic  10 us (2%)
  starting transfers between devices  6.75 us (1%)
    psum x1, waiting for transfers between devices, local(): preactivation_values, adapter_sum = lax.psum((full_acts, down_piece), 'hid')  105 us
    psum x1, blocking collectives, local(): total_rows, total_steer = lax.psum((row_squares, steer_power), 'hid')  96.6 us
    reduce_scatter x1, waiting for transfers between devices, local(): lax.psum_scatter(jnp.einsum('tkf,kdf->td', activation_gradient, weights,...  60.1 us
    all_gather x1, blocking collectives, local(): incoming_gradient = lax.all_gather(cotangent, 'hid', axis=0, tiled=True)  51.5 us
    psum x1, blocking collectives, local(): preactivation_values, adapter_sum = lax.psum((full_acts, down_piece), 'hid')  49.3 us
    psum x1, blocking collectives, local(): back_sum = lax.psum(backward_piece, 'ffn')  46.8 us
    psum x1, blocking collectives, local(): lax.psum(jnp.sum(steered * norm_gain_vector[None, :] * normalized_gradien...  27.5 us
    psum x1, blocking collectives, local(): steered_power = lax.psum(jnp.sum(steered * steered, axis=1), 'hid')  23.7 us
  transfers between devices with their start and end apart: 5, of which 3 were waited for; matrix products, arithmetic and copies ran while one was open for 2% of the time, Pallas kernels for 0%

profile of v1, /device:TPU:1, one launch (start us, length us, event | category | flops | bytes accessed | tf_op | source)
XLA Modules:
  0.0 534.8 jit_solution(4729848772424664306)
XLA Ops:
  7.2 6.6 %pad_maximum_fusion = bf16[2,1,1024,1664]{3,2,1,0:T(8,128)(2,1)} fusion(bf16[1,1,1024,1664]{3,2,1,0:T(8,128)(2,1)} %bitcast.60), kind=kLoop, calls=%fused_computation | loop fusion | flops 3407872 | bytes 10223616 | tf_op jit(solution)/shard_map/stack | solution.py:50
  13.8 6.6 %all-to-all-start = ((bf16[2,1,1024,1664]{3,2,1,0:T(8,128)(2,1)}), bf16[2,1,1024,1664]{3,2,1,0:T(8,128)(2,1)}, u32[]{:S(2)}, u32[]{:S(2)}) async-start(bf16[2,1,1024,1664]{3,2,1,0:T(8,128)(2,1)} %pad_maximum_fusion), calls=%async_computation | async-start | bytes 13631488 | tf_op jit(solution)/shard_map/all_to_all | solution.py:50
  21.2 96.6 %all-reduce = (f32[256]{0:T(256)S(1)}, f32[]{:T(128)}) all-reduce(f32[256]{0:T(256)S(1)} %fusion.15, f32[]{:T(128)} %multiply_reduce_fusion.3), channel_id=1, replica_groups=mesh['dp'=2,'ffn'=16,'hid'=16] {'hid'}, use_global_device_ids=true, to_apply=%region_1.0 | all-reduce | flops 257 | bytes 2056 | tf_op jit(solution)/shard_map/psum | solution.py:38
  118.8 23.7 %psum.72 = f32[256]{0:T(256)S(1)} all-reduce(f32[256]{0:T(256)S(1)} %multiply_reduce_fusion.2), channel_id=1, replica_groups=mesh['dp'=2,'ffn'=16,'hid'=16] {'hid'}, use_global_device_ids=true, to_apply=%region_5.0 | all-reduce | flops 256 | bytes 2048 | tf_op jit(solution)/shard_map/psum | solution.py:43
  142.7 6.7 %fusion.2 = f32[256,2,1664]{2,0,1:T(8,128)} fusion(bf16[2,1,1024,1664]{3,2,1,0:T(8,128)(2,1)} %all-to-all-done, bf16[256,1024]{1,0:T(8,128)(2,1)S(1)} %multiply_convert_fusion), kind=kOutput, calls=%fused_computation.3 | convolution fusion | flops 1744830464 | bytes 10747904 | tf_op jit(solution)/shard_map/td,kdf->tkf/dot_general | solution.py:52
  150.5 49.3 %psum.74 = bf16[256,2,16]{0,2,1:T(8,128)(2,1)S(1)} all-reduce(f32[256,2,16]{0,2,1:T(8,128)S(1)} %bitcast.62), channel_id=1, replica_groups=mesh['dp'=2,'ffn'=16,'hid'=16] {'hid'}, use_global_device_ids=true, to_apply=%region_7.0 | all-reduce | flops 8192 | bytes 49152 | tf_op jit(solution)/shard_map/psum | solution.py:55
  199.8 51.5 %all_gather.6 = bf16[256,1664]{1,0:T(8,128)(2,1)S(1)} all-gather(bf16[16,1664]{1,0:T(8,128)(2,1)S(1)} %copy-done.6), channel_id=1, replica_groups=mesh['dp'=2,'ffn'=16,'hid'=16] {'hid'}, dimensions={0}, use_global_device_ids=true | all-gather | bytes 905216 | tf_op jit(solution)/shard_map/all_gather | solution.py:56
  251.3 105.3 %all-reduce.5.cloned.1.call-done = f32[256,2,1664]{2,0,1:T(8,128)} async-done(((f32[256,2,1664]{2,0,1:T(8,128)}), f32[256,2,1664]{2,0,1:T(8,128)}) %all-reduce.5.cloned.1.call-update) | async-done | bytes 3407888 | tf_op jit(solution)/shard_map/psum | solution.py:55
  356.6 2.6 bitcast_add_fusion
  359.2 0.9 fusion.17
  360.1 1.0 copy-done.2
  361.0 5.9 %fusion.9 = f32[256,1024]{1,0:T(8,128)} fusion(bf16[2,1,1024,1664]{3,2,1,0:T(8,128)(2,1)} %all-to-all-done, bf16[256,1,1664]{2,0,1:T(8,128)(2,1)S(1)} %get-tuple-element.11, bf16[256,1,1664]{2,0,1:T(8,128)(2,1)S(1)} %get-tuple-element.10), kind=kOutput, calls=%fused_computation.18 | convolution fusion | flops 1745682432 | bytes 9568256 | tf_op jit(solution)/shard_map/tkf,kdf->td/dot_general | solution.py:62
  367.0 60.1 %reduce-scatter.2.cloned.1.call-done = f32[16,1024]{1,0:T(8,128)} async-done(((f32[256,1024]{1,0:T(8,128)}), f32[16,1024]{1,0:T(8,128)}) %reduce-scatter.2.cloned.1.call-update) | async-done | bytes 65552 | tf_op jit(solution)/shard_map/reduce_scatter | solution.py:61
  427.2 1.7 convolution_bitcast_fusion.1
  428.9 46.8 %psum.75 = bf16[256,2,16]{0,2,1:T(8,128)(2,1)S(1)} all-reduce(f32[256,2,16]{0,2,1:T(8,128)S(1)} %convolution_bitcast_fusion.1), channel_id=1, replica_groups=mesh['dp'=2,'ffn'=16,'hid'=16] {'ffn'}, use_global_device_ids=true, to_apply=%region_9.0 | all-reduce | flops 8192 | bytes 49152 | tf_op jit(solution)/shard_map/psum | solution.py:71
  475.7 1.1 convolution_multiply_fusion
  476.7 0.9 fusion.14
  477.7 1.7 multiply_reduce_fusion.1
  479.4 27.5 %psum.76 = f32[256]{0:T(256)S(1)} all-reduce(f32[256]{0:T(256)S(1)} %get-tuple-element.12), channel_id=1, replica_groups=mesh['dp'=2,'ffn'=16,'hid'=16] {'hid'}, use_global_device_ids=true, to_apply=%region_11.0 | all-reduce | flops 256 | bytes 2048 | tf_op jit(solution)/shard_map/psum | solution.py:77
  506.9 1.2 multiply_reduce_fusion
  508.1 5.9 %psum.77 = f32[1024]{0:T(1024)} all-reduce(f32[1024]{0:T(1024)S(1)} %get-tuple-element.8), channel_id=1, replica_groups=mesh['dp'=2,'ffn'=16,'hid'=16] {'dp'}, use_global_device_ids=true, to_apply=%region_13.0 | all-reduce | flops 1024 | bytes 8192 | tf_op jit(solution)/shard_map/psum | solution.py:92
  513.9 11.1 %all-reduce.7.cloned.1.call-done = (f32[2,1024,16]{1,2,0:T(8,128)}, f32[2,16,1664]{2,1,0:T(8,128)}) async-done(((f32[2,1024,16]{1,2,0:T(8,128)}, f32[2,16,1664]{2,1,0:T(8,128)}), (f32[2,1024,16]{1,2,0:T(8,128)}, f32[2,16,1664]{2,1,0:T(8,128)})) %all-reduce.7.cloned.1.call-update) | async-done | bytes 344080 | tf_op jit(solution)/shard_map/psum | solution.py:92
  525.1 1.6 copy.15
  526.6 1.6 copy.16
  (35 shorter events, 2.7 us)
Async XLA Ops:
  7.2 349.4 %copy-start = (bf16[2,16,1664]{2,1,0:T(8,128)(2,1)S(1)}, bf16[2,16,1664]{2,1,0:T(8,128)(2,1)}, u32[]{:S(2)}) copy-start(bf16[2,16,1664]{2,1,0:T(8,128)(2,1)} %param.14) | copy-start | bytes 319492
  13.7 6.7 %copy-start.5 = (f32[1024]{0:T(1024)S(1)}, f32[1024]{0:T(1024)}, u32[]{:S(2)}) copy-start(f32[1024]{0:T(1024)} %param.9) | copy-start | bytes 12292
  13.7 7.3 %copy-start.1 = (bf16[256,1024]{1,0:T(8,128)(2,1)S(1)}, bf16[256,1024]{1,0:T(8,128)(2,1)}, u32[]{:S(2)}) copy-start(bf16[256,1024]{1,0:T(8,128)(2,1)} %param.8) | copy-start | bytes 1572868
  13.7 104.7 %copy-start.8 = (f32[256]{0:T(256)S(1)}, f32[256]{0:T(256)}, u32[]{:S(2)}) copy-start(f32[256]{0:T(256)} %param.10) | copy-start | bytes 3076
  13.7 128.7 %copy-start.7 = (f32[1024]{0:T(1024)S(1)}, f32[1024]{0:T(1024)}, u32[]{:S(2)}) copy-start(f32[1024]{0:T(1024)} %param.11) | copy-start | bytes 12292
  13.8 129.0 %all-to-all-start = ((bf16[2,1,1024,1664]{3,2,1,0:T(8,128)(2,1)}), bf16[2,1,1024,1664]{3,2,1,0:T(8,128)(2,1)}, u32[]{:S(2)}, u32[]{:S(2)}) async-start(bf16[2,1,1024,1664]{3,2,1,0:T(8,128)(2,1)} %pad_maximum_fusion), calls=%async_computation | async-start | bytes 13631488 | tf_op jit(solution)/shard_map/all_to_all | solution.py:50
  20.3 336.2 %all-reduce.5.cloned.1.call-start = ((), (), s32[]{:S(2)}) async-start(), calls=%async_computation.2 | async-start | bytes 6815744 | tf_op jit(solution)/shard_map/psum | solution.py:55
  149.4 0.8 copy-start.4
  149.4 50.3 %copy-start.6 = (bf16[16,1664]{1,0:T(8,128)(2,1)S(1)}, bf16[16,1664]{1,0:T(8,128)(2,1)}, u32[]{:S(2)}) copy-start(bf16[16,1664]{1,0:T(8,128)(2,1)} %param.15) | copy-start | bytes 159748
  149.5 277.6 %reduce-scatter.2.cloned.1.call-start = ((), (), s32[]{:S(2)}) async-start(), calls=%async_computation.3 | async-start | bytes 1114112 | tf_op jit(solution)/shard_map/reduce_scatter | solution.py:61
  360.0 1.0 copy-start.2
  366.9 108.8 %copy-start.3 = (bf16[256,1,1664]{2,0,1:T(8,128)(2,1)S(1)}, bf16[256,1,1664]{2,0,1:T(8,128)(2,1)}, u32[]{:S(2)}) copy-start(bf16[256,1,1664]{2,0,1:T(8,128)(2,1)} %copy-done.2) | copy-start | bytes 2555908
  366.9 110.7 %all-gather.2.cloned.1.call-start = ((), (), s32[]{:S(2)}) async-start(), calls=%async_computation.4 | async-start | bytes 1114112 | tf_op jit(solution)/shard_map/all_gather | solution.py:67
  427.1 97.9 %all-reduce.7.cloned.1.call-start = ((), (), s32[]{:S(2)}) async-start(), calls=%async_computation.5 | async-start | bytes 688128 | tf_op jit(solution)/shard_map/psum | solution.py:92
Sparse Core Ops, SparseCore 0:
  149.6 206.9 all-reduce.4
  367.0 60.0 reduce-scatter.1
  429.2 43.1 all-gather.1
  477.7 47.2 all-reduce.6
